TPU v7x, 32 devices: a whole 2x2x4 slice. The times are simulated.
32 devices in a mesh: groups: 2 (over y), seq: 4 (over z), pair: 2 (over x), sub: 2 (over core).
Axes of the slice: x: 2, y: 2, z: 4, core: 2. Of those that a mesh axis runs over, the one named last changes fastest.
Arguments:
- embeddings: bfloat16 [64, 256, 1024], P(('groups', 'seq'), 'sub'), parts along dimension 0, may hold values from -8 to 8
- pairs: int32 [128, 2], P(('groups', 'seq', 'pair')), parts along dimension 0, may hold values from 0 to 31, as said below
- lengths: int32 [64], P('groups'), parts along dimension 0, may hold values from 64 to 256
Outputs:
- profile: bfloat16 [64, 256, 1024], P(('groups', 'seq'), 'sub', 'pair'), parts along dimension 0
There are 2 independent parts, one for each index of `groups`. A program takes and returns all parts, laid end to end along the dimension named above; each array names one. Nothing has to cross between parts.
Inputs may be any that keep to these rules, and one draw needn't show every extreme that they name: The rows of pairs form 4 * 2 aligned blocks of 8 rows (the rows of one device); in block k every query id (column 0) lies in (k // 2) * 8 to (k // 2 + 1) * 8 - 1, and for every owner j exactly 2 target ids (column 1) lie in j * 8 to (j + 1) * 8 - 1. A target never equals its query.
All inputs are finite; a program needn't handle non-finite values.
Results may differ from a plain program's by a relative error of at most 0.006.
Values may be sent and summed in bfloat16 or wider, within the bound.
A program may use at most 128 MiB of HBM per device.

v0:
```python
import math

import jax
import jax.numpy as jnp
from jax import lax
from jax.sharding import PartitionSpec as P

masked_fill = -1e30


def combined_all(part, axis, combine):
    gathered = jax.tree.map(lambda a: lax.all_gather(a, axis), part)

    def take(source):
        return jax.tree.map(lambda a: lax.dynamic_index_in_dim(a, source, 0, False), gathered)

    return lax.fori_loop(
        1, lax.axis_size(axis), lambda source, state: combine(state, take(source)), take(0)
    )


def slot_ranks(owners):
    count = owners.shape[0]
    same = owners[:, None] == owners[None, :]
    earlier = jnp.arange(count)[:, None] > jnp.arange(count)[None, :]
    return jnp.sum((same & earlier).astype(jnp.int32), axis=1)


def column_combine(first, second):
    col_top = jnp.maximum(first[0], second[0])
    col_total = first[1] * jnp.exp(first[0] - col_top) + second[1] * jnp.exp(second[0] - col_top)
    return (col_top, col_total)


def column_stats(scores, row_valid):
    masked = jnp.where(row_valid, scores, masked_fill)
    col_top = jnp.max(masked, axis=-2, keepdims=True)
    col_total = jnp.sum(
        jnp.where(row_valid, jnp.exp(masked - col_top), 0.0), axis=-2, keepdims=True
    )
    return (col_top, col_total)


def finish_tiles(scores, row_valid, col_valid, col_top, col_total, target_block):
    masked = jnp.where(col_valid, scores, masked_fill)
    row_top = jnp.max(masked, axis=-1, keepdims=True)
    row_exp = jnp.exp(masked - row_top)
    row_soft = row_exp / jnp.sum(row_exp, axis=-1, keepdims=True)
    col_soft = jnp.where(row_valid, jnp.exp(scores - col_top), 0.0) / col_total
    weights = jnp.where(row_valid & col_valid, 0.5 * (row_soft + col_soft), 0.0).astype(
        jnp.bfloat16
    )
    return jnp.einsum(
        "...ij,...jd->...id", weights, target_block, preferred_element_type=jnp.float32
    )


def local(embeddings, pairs, lengths):
    prot_dev, half, width = embeddings.shape
    pair_dev = pairs.shape[0]
    seq_count = lax.axis_size("seq")
    pair_count = lax.axis_size("pair")
    seq_index = lax.axis_index("seq")
    sub_index = lax.axis_index("sub")
    full = half * lax.axis_size("sub")
    capacity = pair_dev // seq_count
    root_width = math.sqrt(width)
    query_ids = pairs[:, 0]
    target_ids = pairs[:, 1]
    query_local = query_ids - seq_index * prot_dev
    target_owner = target_ids // prot_dev
    target_local = target_ids % prot_dev
    target_rank = slot_ranks(target_owner)
    owner_range = jnp.arange(seq_count, dtype=jnp.int32)
    slot_range = jnp.arange(capacity, dtype=jnp.int32)
    own_placed = (target_owner[:, None, None] == owner_range[None, :, None]) & (
        target_rank[:, None, None] == slot_range[None, None, :]
    )
    table = jnp.sum(jnp.where(own_placed, target_local[:, None, None], 0), axis=0)
    wanted = lax.all_to_all(table, "seq", split_axis=0, concat_axis=0, tiled=True)
    outgoing = embeddings[wanted]
    queries = embeddings[query_local]
    query_length = lengths[query_ids]
    target_length = lengths[target_ids]
    row_valid = (sub_index * half + jnp.arange(half))[None, :, None] < query_length[:, None, None]
    col_valid = jnp.arange(full)[None, None, :] < target_length[:, None, None]
    prot_range = jnp.arange(prot_dev, dtype=jnp.int32)
    pooled_sum = None
    arrived = lax.all_to_all(outgoing, "seq", split_axis=0, concat_axis=0, tiled=True)
    arrived_flat = arrived.reshape(seq_count * capacity, half, width)
    picked = arrived_flat[target_owner * capacity + target_rank]
    targets = lax.all_gather(picked, "sub", axis=1, tiled=True)

    def single_tile(running, members):
        query_block, target_block, row_live, col_live, owner_row = members
        scores = (
            jnp.dot(query_block, target_block.T, preferred_element_type=jnp.float32) / root_width
        )
        col_top, col_total = combined_all(column_stats(scores, row_live), "sub", column_combine)
        result = finish_tiles(scores, row_live, col_live, col_top, col_total, target_block)
        current = lax.dynamic_index_in_dim(running, owner_row, 0, keepdims=False)
        running = lax.dynamic_update_index_in_dim(running, current + result, owner_row, 0)
        return (running, None)

    start_sum = jnp.zeros((prot_dev, half, width), jnp.float32)
    pooled_sum, _ = lax.scan(
        single_tile, start_sum, (queries, targets, row_valid, col_valid, query_local)
    )
    owner_hot = (query_local[:, None] == prot_range[None, :]).astype(jnp.float32)
    count_terms = jnp.broadcast_to(
        jnp.sum(owner_hot, axis=0)[:, None, None], (prot_dev, 1, pair_count)
    )
    summed, counted = (
        lax.psum_scatter(
            pooled_sum.astype(jnp.bfloat16), "pair", scatter_dimension=2, tiled=True
        ).astype(jnp.float32),
        lax.psum_scatter(
            count_terms.astype(jnp.bfloat16), "pair", scatter_dimension=2, tiled=True
        ).astype(jnp.float32),
    )
    return (summed / jnp.maximum(counted, 1.0)).astype(jnp.bfloat16)


def solution(mesh):
    placed = (P(("groups", "seq"), "sub", None), P(("groups", "seq", "pair"), None), P("groups"))
    return jax.shard_map(
        local,
        mesh=mesh,
        in_specs=placed,
        out_specs=P(("groups", "seq"), "sub", "pair"),
        check_vma=False,
    )
```

profile of v0, /device:TPU:0, one launch (start us, length us, event | category | flops | bytes accessed | tf_op | source)
XLA Modules:
  0.0 229.4 jit_solution(1787006364183932311)
XLA Ops:
  8.6 11.7 %all_to_all.17 = s32[4,1,2]{2,1,0:T(1,128)S(1)} all-to-all(s32[4,1,2]{2,1,0:T(1,128)S(1)} %copy.9), channel_id=1, replica_groups=mesh['groups'=2,'seq'=4,'pair'=2,'sub'=2] {'seq'}, dimensions={0} | all-to-all | bytes 64 | tf_op jit(solution)/shard_map/all_to_all | solution.py:80
  20.5 2.0 gather_fusion.3
  22.5 4.4 %all-to-all-start.1 = ((bf16[4,2,128,1024]{3,2,1,0:T(8,128)(2,1)}), bf16[4,2,128,1024]{3,2,1,0:T(8,128)(2,1)}, u32[]{:S(2)}, u32[]{:S(2)}) async-start(bf16[4,2,128,1024]{3,2,1,0:T(8,128)(2,1)} %bitcast.94), calls=%async_computation.1 | async-start | bytes 4194304 | tf_op jit(solution)/shard_map/all_to_all | solution.py:89
  27.0 47.0 %all-to-all-done.1 = bf16[4,2,128,1024]{3,2,1,0:T(8,128)(2,1)} async-done(((bf16[4,2,128,1024]{3,2,1,0:T(8,128)(2,1)}), bf16[4,2,128,1024]{3,2,1,0:T(8,128)(2,1)}, u32[]{:S(2)}, u32[]{:S(2)}) %all-to-all-start.1) | async-done | bytes 2097184 | tf_op jit(solution)/shard_map/all_to_all | solution.py:89
  74.1 3.6 %gather_fusion.4 = bf16[8,128,1024]{2,1,0:T(8,128)(2,1)} fusion(bf16[8,128,1024]{2,1,0:T(8,128)(2,1)} %bitcast.21, s32[1024]{0:T(1024)S(1)} %pad_clamp_fusion), kind=kCustom, calls=%fused_computation.4 | custom fusion | bytes 4194336 | tf_op jit(solution)/shard_map/gather | solution.py:91
  79.6 2.1 gather_fusion.2
  81.9 8.8 %all-gather.11.cloned.1.call-done = bf16[8,256,1024]{2,1,0:T(8,128)(2,1)} async-done(((bf16[8,128,1024]{2,1,0:T(8,128)(2,1)}), bf16[8,256,1024]{2,1,0:T(8,128)(2,1)}) %all-gather.11.cloned.1.call-update) | async-done | bytes 4194320 | tf_op jit(solution)/shard_map/all_gather | solution.py:92
  90.6 2.5 %broadcast_in_dim.59 = f32[8,128,1024]{2,1,0:T(8,128)} broadcast(f32[]{:T(128)} %constant.91.clone.1), dimensions={} | broadcast | bytes 4194308 | tf_op jit(solution)/shard_map/broadcast_in_dim | solution.py:105
  93.1 89.7 %while.12 = (s32[]{:T(128)}, f32[8,128,1024]{2,1,0:T(8,128)}, s32[8]{0:T(128)S(1)}, pred[8,128,1]{1,2,0:T(4,128)(4,1)S(1)}, pred[8,1,256]{2,1,0:T(4,128)(4,1)S(1...) while((s32[]{:T(128)}, f32[8,128,1024]{2,1,0:T(8,128)}, ...), condition=%wide.region_7.8_spmd, body=%wide.region_2.7_spmd.sunk | while | flops 135103232 | bytes 3832867 | solution.py:106
  93.2 1.5 select_reduce_fusion.5
  94.9 1.8 all-gather.7
  96.7 1.8 all-gather.8
  101.1 1.1 constant_dynamic-slice_fusion.2
  102.2 2.1 fusion.41
  104.4 1.5 select_reduce_fusion.5
  106.1 1.8 all-gather.7
  107.9 1.8 all-gather.8
  112.3 1.1 constant_dynamic-slice_fusion.2
  113.4 2.1 fusion.41
  115.6 1.5 select_reduce_fusion.5
  117.3 1.8 all-gather.7
  119.1 1.8 all-gather.8
  124.6 2.1 fusion.41
  126.8 1.5 select_reduce_fusion.5
  128.5 1.8 all-gather.7
  130.3 1.8 all-gather.8
  135.8 2.1 fusion.41
  138.0 1.5 select_reduce_fusion.5
  139.7 1.8 all-gather.7
  141.5 1.8 all-gather.8
  147.0 2.1 fusion.41
  149.2 1.5 select_reduce_fusion.5
  150.9 1.8 all-gather.7
  152.7 1.8 all-gather.8
  158.2 2.2 fusion.41
  160.4 1.5 select_reduce_fusion.5
  162.1 1.8 all-gather.7
  163.9 1.8 all-gather.8
  168.4 1.1 constant_dynamic-slice_fusion.2
  169.5 2.2 fusion.41
  171.7 1.5 select_reduce_fusion.5
  173.4 1.8 all-gather.7
  175.2 1.8 all-gather.8
  180.7 2.2 fusion.41
  182.9 3.9 %convert_element_type.31 = bf16[8,128,1024]{2,1,0:T(8,128)(2,1)} convert(f32[8,128,1024]{2,1,0:T(8,128)} %get-tuple-element.60) | non-fusion elementwise | flops 1048576 | bytes 6291456 | tf_op jit(solution)/shard_map/convert_element_type | solution.py:115
  186.8 4.9 %all-reduce = bf16[8,1,2]{0,2,1:T(2,128)(2,1)S(1)} all-reduce(bf16[8,1,2]{0,2,1:T(2,128)(2,1)S(1)} %broadcast_in_dim.62), channel_id=6, replica_groups=mesh['groups'=2,'seq'=4,'pair'=2,'sub'=2] {'pair'}, use_global_device_ids=true, to_apply=%region_10.11.clone | all-reduce | flops 16 | bytes 64
  193.0 27.0 %reduce-scatter.3.cloned.1.call-done = bf16[8,128,512]{2,1,0:T(8,128)(2,1)} async-done(((bf16[8,128,1024]{2,1,0:T(8,128)(2,1)}), bf16[8,128,512]{2,1,0:T(8,128)(2,1)}) %reduce-scatter.3.cloned.1.call-update) | async-done | bytes 1048592 | tf_op jit(solution)/shard_map/reduce_scatter | solution.py:114
  220.0 2.6 %divide_convert_fusion = bf16[8,128,512]{2,1,0:T(8,128)(2,1)} fusion(bf16[8,128,512]{2,1,0:T(8,128)(2,1)} %reduce-scatter.3.cloned.1.call-done, f32[8]{0:T(128)S(1)} %fusion.29), kind=kLoop, calls=%fused_computation.39 | loop fusion | flops 1572864 | bytes 2097184 | tf_op jit(solution)/shard_map/convert_element_type | solution.py:121
  (97 shorter events, 18.3 us)
Async XLA Ops:
  6.5 14.0 %copy-start = (bf16[8,128,1024]{2,1,0:T(8,128)(2,1)S(1)}, bf16[8,128,1024]{2,1,0:T(8,128)(2,1)}, u32[]{:S(2)}) copy-start(bf16[8,128,1024]{2,1,0:T(8,128)(2,1)} %param.5) | copy-start | bytes 6291460
  22.5 51.6 %all-to-all-start.1 = ((bf16[4,2,128,1024]{3,2,1,0:T(8,128)(2,1)}), bf16[4,2,128,1024]{3,2,1,0:T(8,128)(2,1)}, u32[]{:S(2)}, u32[]{:S(2)}) async-start(bf16[4,2,128,1024]{3,2,1,0:T(8,128)(2,1)} %bitcast.94), calls=%async_computation.1 | async-start | bytes 4194304 | tf_op jit(solution)/shard_map/all_to_all | solution.py:89
  27.0 63.7 %all-gather.11.cloned.1.call-start = ((), (), s32[]{:S(2)}) async-start(), calls=%async_computation.4 | async-start | bytes 6291456 | tf_op jit(solution)/shard_map/all_gather | solution.py:92
  77.7 0.7 copy-start.1
  77.7 142.3 %reduce-scatter.3.cloned.1.call-start = ((), (), s32[]{:S(2)}) async-start(), calls=%async_computation.3 | async-start | bytes 3145728 | tf_op jit(solution)/shard_map/reduce_scatter | solution.py:114
  186.7 5.1 %copy-start.2 = (u32[32]{0:T(128)S(1)}, u32[32]{0:T(128)}, u32[]{:S(2)}) copy-start(u32[32]{0:T(128)} %constant.107) | copy-start | bytes 388
Sparse Core Ops, SparseCore 0:
  77.8 12.7 all-gather.10
  186.9 33.0 reduce-scatter.2
where the time goes:
time: 231 us; the launch traced here: 229 us
  waiting for transfers between devices  82.8 us (36%)
  blocking collectives  45 us (19%)
  matrix products  29.4 us (13%)
  local copies, waits for them, and re-layouts  27 us (12%)
  loops' own time  16.2 us (7%)
  between operations  13.5 us (6%)
  other arithmetic  11 us (5%)
  starting transfers between devices  4.52 us (2%)
    all_to_all x1, waiting for transfers between devices, local(): lax.all_to_all(outgoing, 'seq', split_axis=0, concat_axis=0, tiled=True)  47 us
    all_gather x16, blocking collectives, combined_all(): gathered = jax.tree.map(lambda a: lax.all_gather(a, axis), part)  28.4 us
    reduce_scatter x1, waiting for transfers between devices, local(): lax.psum_scatter(pooled_sum.astype(jnp.bfloat16), 'pair', scatter_dimensi...  27 us
    dot_general x8, matrix products, finish_tiles(): jnp.einsum('...ij,...jd->...id', weights, target_block, preferred_element...  17.3 us
    another operation x1, loops' own time, local(): lax.scan(single_tile, start_sum, (queries, targets, row_valid, col_valid,...  16.2 us
    dot_general x8, matrix products, single_tile(): jnp.dot(query_block, target_block.T, preferred_element_type=jnp.float32)  12.1 us
    all_to_all x1, blocking collectives, local(): lax.all_to_all(table, 'seq', split_axis=0, concat_axis=0, tiled=True)  11.7 us
    all_gather x1, waiting for transfers between devices, local(): targets = lax.all_gather(picked, 'sub', axis=1, tiled=True)  8.76 us
  transfers between devices with their start and end apart: 3, of which 3 were waited for; matrix products, arithmetic and copies ran while one was open for 2% of the time, Pallas kernels for 0%

commit v1 on v0

v1 whole, which is shorter than its diff:
```python
import functools
import math

import jax
import jax.numpy as jnp
from jax import lax
from jax.experimental import pallas as pl
from jax.experimental.pallas import tpu as pltpu
from jax.sharding import PartitionSpec as P

masked_fill = -1e30
MESH = pl.DeviceIdType.MESH


def kernel(
    seq_count,
    pair_count,
    pairs_ref,
    pairs_vmem,
    lengths_ref,
    emb_ref,
    out_ref,
    info_seq_vmem,
    info_pair_vmem,
    info_seq,
    info_pair,
    query_table,
    target_table,
    other_query_table,
    emb_other,
    outgoing,
    t_own,
    t_other,
    w_own,
    w_other,
    acc,
    seq_info_send,
    seq_info_recv,
    pair_info_send,
    pair_info_recv,
    query_send,
    query_recv,
    smem_sem,
    z_send,
    z_recv,
    s_send,
    s_recv,
    xt_send,
    xt_recv,
    xs_send,
    xs_recv,
    xw_send,
    xw_recv,
):
    me = lax.axis_index("seq")
    mine = lax.axis_index("pair")
    sub = lax.axis_index("sub")
    sibling = 1 - sub
    prot_dev, half, width = emb_ref.shape
    full = 2 * half
    pair_dev = pairs_ref.shape[0]
    capacity = pair_dev // seq_count
    slots = pair_dev
    features = width // pair_count
    own_rows = pl.ds(pl.multiple_of(sub * half, half), half)
    sibling_rows = pl.ds(pl.multiple_of(sibling * half, half), half)
    own_features = pl.ds(pl.multiple_of(mine * features, features), features)

    def seq_peer(distance):
        return {"seq": lax.rem(me + distance, seq_count)}

    def pair_peer(distance):
        return {"pair": lax.rem(mine + distance, pair_count)}

    def remote(src, dst, send, recv, device):
        return pltpu.make_async_remote_copy(
            src_ref=src, dst_ref=dst, send_sem=send, recv_sem=recv, device_id=device,
            device_id_type=MESH,
        )

    def seq_info_copy(d):
        return remote(
            pairs_vmem, info_seq_vmem.at[d - 1], seq_info_send.at[d - 1], seq_info_recv.at[d - 1],
            seq_peer(d),
        )

    def pair_info_copy(d):
        there = pair_count - d - 1
        return remote(
            pairs_vmem, info_pair_vmem.at[there], pair_info_send.at[there],
            pair_info_recv.at[there], pair_peer(d),
        )

    def query_copy():
        return remote(emb_ref, emb_other, query_send, query_recv, {"sub": sibling})

    def z_copy(d, i):
        return remote(
            outgoing.at[i - capacity], t_own.at[i, own_rows, :], z_send.at[i], z_recv.at[i],
            seq_peer(d),
        )

    def s_copy(i, rows):
        return remote(
            t_own.at[i, rows, :], t_own.at[i, rows, :], s_send.at[i], s_recv.at[i],
            {"sub": sibling},
        )

    def xt_copy(d, i):
        there = pair_count - d - 1
        peer = lax.rem(mine + d, pair_count)
        columns = pl.ds(pl.multiple_of(peer * features, features), features)
        return remote(
            t_own.at[i, own_rows, columns], t_other.at[there, i, own_rows, :],
            xt_send.at[there, i], xt_recv.at[there, i], pair_peer(d),
        )

    def xs_copy(e, i, rows):
        return remote(
            t_other.at[e, i, rows, :], t_other.at[e, i, rows, :], xs_send.at[e, i],
            xs_recv.at[e, i], {"sub": sibling},
        )

    def xw_copy(d, i):
        there = pair_count - d - 1
        return remote(
            w_own.at[i], w_other.at[there, i], xw_send.at[there, i], xw_recv.at[there, i],
            pair_peer(d),
        )

    barrier = pltpu.get_barrier_semaphore()
    for d in range(1, seq_count):
        pl.semaphore_signal(barrier, inc=1, device_id=seq_peer(d), device_id_type=MESH)
    for d in range(1, pair_count):
        pl.semaphore_signal(barrier, inc=1, device_id=pair_peer(d), device_id_type=MESH)
    pl.semaphore_signal(barrier, inc=1, device_id={"sub": sibling}, device_id_type=MESH)
    pl.semaphore_wait(barrier, seq_count + pair_count - 1)

    for d in range(1, seq_count):
        seq_info_copy(d).start()
    for d in range(1, pair_count):
        pair_info_copy(d).start()
    query_copy().start()

    def find(table, owner, rank):
        def look(n, state):
            seen, query, target = state
            query_id = table[n, 0]
            target_id = table[n, 1]
            match = lax.div(target_id, prot_dev) == owner
            take = jnp.logical_and(match, seen == rank)
            query = jnp.where(take, query_id, query)
            target = jnp.where(take, target_id, target)
            seen = seen + jnp.where(match, 1, 0)
            return (seen, query, target)

        zero = jnp.int32(0)
        _, query, target = lax.fori_loop(0, pair_dev, look, (zero, zero, zero))
        return query, target

    for d in range(1, seq_count):
        seq_info_copy(d).wait_recv()
    for d in range(1, pair_count):
        pair_info_copy(d).wait_recv()
    local_seq = pltpu.make_async_copy(info_seq_vmem, info_seq, smem_sem.at[0])
    local_pair = pltpu.make_async_copy(info_pair_vmem, info_pair, smem_sem.at[1])
    local_seq.start()
    local_pair.start()
    local_seq.wait()
    local_pair.wait()

    def send_targets(step, carry):
        d = lax.div(step, capacity) + 1
        rank = lax.rem(step, capacity)
        asker = info_seq.at[seq_count - d - 1]
        _, target = find(asker, me, rank)
        outgoing[step] = emb_ref[lax.rem(target, prot_dev)]
        z_copy(d, step + capacity).start()
        return carry

    lax.fori_loop(0, slots - capacity, send_targets, 0)

    def fill_tables(i, carry):
        d = lax.div(i, capacity)
        rank = lax.rem(i, capacity)
        owner = lax.rem(me - d + seq_count, seq_count)
        query, target = find(pairs_ref, owner, rank)
        query_table[i] = lax.rem(query, prot_dev)
        target_table[i] = target

        def others(e, inner):
            other_query, _ = find(info_pair.at[e], owner, rank)
            other_query_table[e, i] = lax.rem(other_query, prot_dev)
            return inner

        return lax.fori_loop(0, pair_count - 1, others, carry)

    lax.fori_loop(0, slots, fill_tables, 0)

    def own_targets(i, carry):
        t_own[i, own_rows, :] = emb_ref[lax.rem(target_table[i], prot_dev)]
        return carry

    lax.fori_loop(0, capacity, own_targets, 0)
    acc[...] = jnp.zeros_like(acc)
    query_copy().wait_recv()

    scale = 1.0 / math.sqrt(width)
    contract = (((1,), (1,)), ((), ()))

    def weights(i):
        query = query_table[i]
        target = target_table[i]
        query_length = lengths_ref[query + me * prot_dev]
        target_length = lengths_ref[target]
        block = t_own[i]
        own = scale * lax.dot_general(
            emb_ref[query], block, contract, preferred_element_type=jnp.float32
        )
        other = scale * lax.dot_general(
            emb_other[query], block, contract, preferred_element_type=jnp.float32
        )
        rows = lax.broadcasted_iota(jnp.int32, (half, full), 0)
        columns = lax.broadcasted_iota(jnp.int32, (half, full), 1)
        own_live = rows + sub * half < query_length
        other_live = rows + sibling * half < query_length
        col_live = columns < target_length
        col_top = jnp.maximum(
            jnp.max(jnp.where(own_live, own, masked_fill), axis=0, keepdims=True),
            jnp.max(jnp.where(other_live, other, masked_fill), axis=0, keepdims=True),
        )
        own_exp = jnp.where(own_live, jnp.exp(own - col_top), 0.0)
        other_exp = jnp.where(other_live, jnp.exp(other - col_top), 0.0)
        col_total = jnp.sum(own_exp, axis=0, keepdims=True) + jnp.sum(
            other_exp, axis=0, keepdims=True
        )
        masked = jnp.where(col_live, own, masked_fill)
        row_exp = jnp.exp(masked - jnp.max(masked, axis=1, keepdims=True))
        row_total = jnp.sum(row_exp, axis=1, keepdims=True)
        both = row_exp * (0.5 / row_total) + own_exp * (0.5 / col_total)
        w_own[i] = jnp.where(jnp.logical_and(own_live, col_live), both, 0.0).astype(jnp.bfloat16)

    def add(weight, block, query):
        result = jnp.dot(weight, block, preferred_element_type=jnp.float32)
        for a in range(prot_dev):
            acc[a] += jnp.where(query == a, result, 0.0)

    def step(i, carry):
        @pl.when(i < slots)
        def _():
            @pl.when(i >= capacity)
            def _():
                z_copy(1, i).wait_recv()

            s_copy(i, own_rows).start()
            for d in range(1, pair_count):
                xt_copy(d, i).start()

        @pl.when(jnp.logical_and(i >= 1, i <= slots))
        def _():
            k = i - 1
            for e in range(pair_count - 1):
                xt_copy(pair_count - 1 - e, k).wait_recv()
                xs_copy(e, k, own_rows).start()
            s_copy(k, sibling_rows).wait_recv()
            weights(k)
            for d in range(1, pair_count):
                xw_copy(d, k).start()
            add(w_own[k], t_own[k, :, own_features], query_table[k])

        @pl.when(i >= 2)
        def _():
            k = i - 2

            def remote_add(e, inner):
                xw_copy(pair_count - 1 - e, k).wait_recv()
                xs_copy(e, k, sibling_rows).wait_recv()
                add(w_other[e, k], t_other[e, k], other_query_table[e, k])
                return inner

            lax.fori_loop(0, pair_count - 1, remote_add, 0)

        return carry

    lax.fori_loop(0, slots + 2, step, 0)

    def count_of(table, start):
        def look(n, counts):
            query = lax.rem(table[n, 0], prot_dev)
            return tuple(c + jnp.where(query == a, 1, 0) for a, c in enumerate(counts))

        return lax.fori_loop(0, pair_dev, look, start)

    counts = count_of(pairs_ref, (jnp.int32(0),) * prot_dev)
    counts = lax.fori_loop(
        0, pair_count - 1, lambda e, state: count_of(info_pair.at[e], state), counts
    )
    for a in range(prot_dev):
        divisor = jnp.maximum(counts[a], 1).astype(jnp.float32)
        out_ref[a] = (acc[a] / divisor).astype(out_ref.dtype)

    for d in range(1, seq_count):
        seq_info_copy(d).wait_send()
    for d in range(1, pair_count):
        pair_info_copy(d).wait_send()
    query_copy().wait_send()

    def finish(i, carry):
        @pl.when(i >= capacity)
        def _():
            z_copy(1, i).wait_send()

        s_copy(i, own_rows).wait_send()
        for d in range(1, pair_count):
            xt_copy(d, i).wait_send()
            xs_copy(d - 1, i, own_rows).wait_send()
            xw_copy(d, i).wait_send()
        return carry

    lax.fori_loop(0, slots, finish, 0)


def local(seq_count, pair_count, embeddings, pairs, lengths):
    prot_dev, half, width = embeddings.shape
    pair_dev = pairs.shape[0]
    full = 2 * half
    features = width // pair_count
    capacity = pair_dev // seq_count
    others = pair_count - 1
    smem = pl.BlockSpec(memory_space=pltpu.SMEM)
    vmem = pl.BlockSpec(memory_space=pltpu.VMEM)
    dma = pltpu.SemaphoreType.DMA
    bf16 = jnp.bfloat16
    return pl.pallas_call(
        functools.partial(kernel, seq_count, pair_count),
        out_shape=jax.ShapeDtypeStruct((prot_dev, half, features), bf16),
        in_specs=[smem, vmem, smem, vmem],
        out_specs=vmem,
        scratch_shapes=[
            pltpu.VMEM((seq_count - 1, pair_dev, 2), jnp.int32),
            pltpu.VMEM((others, pair_dev, 2), jnp.int32),
            pltpu.SMEM((seq_count - 1, pair_dev, 2), jnp.int32),
            pltpu.SMEM((others, pair_dev, 2), jnp.int32),
            pltpu.SMEM((pair_dev,), jnp.int32),
            pltpu.SMEM((pair_dev,), jnp.int32),
            pltpu.SMEM((others, pair_dev), jnp.int32),
            pltpu.VMEM((prot_dev, half, width), bf16),
            pltpu.VMEM((pair_dev - capacity, half, width), bf16),
            pltpu.VMEM((pair_dev, full, width), bf16),
            pltpu.VMEM((others, pair_dev, full, features), bf16),
            pltpu.VMEM((pair_dev, half, full), bf16),
            pltpu.VMEM((others, pair_dev, half, full), bf16),
            pltpu.VMEM((prot_dev, half, features), jnp.float32),
            dma((seq_count - 1,)),
            dma((seq_count - 1,)),
            dma((others,)),
            dma((others,)),
            dma,
            dma,
            dma((2,)),
            dma((pair_dev,)),
            dma((pair_dev,)),
            dma((pair_dev,)),
            dma((pair_dev,)),
            dma((others, pair_dev)),
            dma((others, pair_dev)),
            dma((others, pair_dev)),
            dma((others, pair_dev)),
            dma((others, pair_dev)),
            dma((others, pair_dev)),
        ],
        compiler_params=pltpu.CompilerParams(
            collective_id=0, has_side_effects=True, vmem_limit_bytes=60 * 1024 * 1024
        ),
    )(pairs, pairs, lengths, embeddings)


def solution(mesh):
    placed = (P(("groups", "seq"), "sub", None), P(("groups", "seq", "pair"), None), P("groups"))
    return jax.shard_map(
        functools.partial(local, mesh.shape["seq"], mesh.shape["pair"]),
        mesh=mesh,
        in_specs=placed,
        out_specs=P(("groups", "seq"), "sub", "pair"),
        check_vma=False,
    )
```

time: 231 us -> 76.6 us (0.33)
  the two profiles are of different devices: /device:TPU:0 before, /device:TPU:28 now
where the time goes in v1:
time: 76.6 us; the launch traced here: 76.4 us
  Pallas kernels  72.7 us (95%)
  local copies, waits for them, and re-layouts  3.61 us (5%)
    pallas_call x1, Pallas kernels, local(): pl.pallas_call(functools.partial(kernel, seq_count, pair_count), out_shap...  72.7 us
    unnamed x2, local copies, waits for them, and re-layouts  3.61 us

profile of v1, /device:TPU:28, one launch (start us, length us, event | category | flops | bytes accessed | tf_op | source)
XLA Modules:
  0.0 76.4 jit_solution(6030972583372019537)
XLA Ops:
  0.0 1.3 %copy.4.pairs_ref.pairs_vmem = s32[8,2]{1,0:T(8,128)} copy(s32[8,2]{0,1:T(2,128)} %param.4) | data formatting | bytes 128 | tf_op args[1]
  1.3 72.7 %shard_map.37 = bf16[8,128,512]{2,1,0:T(8,128)(2,1)} custom-call(s32[8,2]{1,0:T(8,128)} %copy.4.pairs_ref.pairs_vmem, s32[8,2]{1,0:T(8,128)} %copy.4.pairs_ref.pairs_vmem, s32[32]{0:T(128)} %lengths_ref.1, bf16[8,128,1024]{2,1,0:T(8,128)(2,1)} %emb_ref.1), custom_call_target="tpu_custom_call" | custom-call | tf_op jit(solution)/shard_map/pallas_call | solution.py:334
  74.1 2.3 %copy.7 = bf16[8,128,512]{2,1,0:T(8,128)(2,1)} copy(bf16[8,128,512]{2,1,0:T(8,128)(2,1)} %shard_map.37) | data formatting | bytes 2097152

commit v2 on v1

v2 whole, which is shorter than its diff:
```python
import functools
import math

import jax
import jax.numpy as jnp
from jax import lax
from jax.experimental import pallas as pl
from jax.experimental.pallas import tpu as pltpu
from jax.sharding import PartitionSpec as P

masked_fill = -1e30
window = 2
lag = 1
shift = 0
MESH = pl.DeviceIdType.MESH


def kernel(
    seq_count,
    pair_count,
    pairs_ref,
    lengths_ref,
    emb_hbm,
    out_ref,
    table,
    seq_tables,
    pair_tables,
    emb_ref,
    emb_other,
    outgoing,
    t_own,
    r_out,
    r_in,
    acc,
    load_sem,
    seq_info_send,
    seq_info_recv,
    pair_info_send,
    pair_info_recv,
    query_send,
    query_recv,
    z_send,
    z_recv,
    s_send,
    s_recv,
    x_send,
    x_recv,
):
    me = lax.axis_index("seq")
    mine = lax.axis_index("pair")
    sub = lax.axis_index("sub")
    sibling = 1 - sub
    prot_dev, half, width = emb_ref.shape
    full = 2 * half
    pair_dev = pairs_ref.shape[1]
    capacity = pair_dev // seq_count
    slots = pair_dev
    features = width // pair_count
    own_rows = pl.ds(pl.multiple_of(sub * half, half), half)
    sibling_rows = pl.ds(pl.multiple_of(sibling * half, half), half)

    def slot_key(i):
        j = i - capacity
        later = i >= capacity
        d = jnp.where(later, lax.rem(j + shift, seq_count - 1) + 1, 0)
        rank = jnp.where(later, lax.div(j, seq_count - 1), i)
        return d, rank

    def partner(d):
        result = jnp.int32(0)
        bit = 1
        while bit < seq_count:
            result += lax.rem(lax.div(me, bit) + lax.div(jnp.int32(d), bit), 2) * bit
            bit *= 2
        return result

    def seq_peer(d):
        return {"seq": partner(d)}

    def pair_peer(distance):
        return {"pair": lax.rem(mine + distance, pair_count)}

    def feature_block(index):
        return pl.ds(pl.multiple_of(index * features, features), features)

    def remote(src, dst, send, recv, device):
        return pltpu.make_async_remote_copy(
            src_ref=src, dst_ref=dst, send_sem=send, recv_sem=recv, device_id=device,
            device_id_type=MESH,
        )

    def seq_info_copy(d):
        return remote(
            table, seq_tables.at[d - 1], seq_info_send.at[d - 1], seq_info_recv.at[d - 1],
            seq_peer(d),
        )

    def pair_info_copy(d):
        there = pair_count - d - 1
        return remote(
            table, pair_tables.at[there], pair_info_send.at[there], pair_info_recv.at[there],
            pair_peer(d),
        )

    def query_copy():
        return remote(emb_ref, emb_other, query_send, query_recv, {"sub": sibling})

    def z_copy(d, i):
        return remote(
            outgoing.at[i - capacity], t_own.at[i, own_rows, :], z_send.at[i - capacity],
            z_recv.at[i - capacity], seq_peer(d),
        )

    def s_copy(i, rows):
        return remote(
            t_own.at[i, rows, :], t_own.at[i, rows, :], s_send.at[i - capacity],
            s_recv.at[i - capacity], {"sub": sibling},
        )

    def x_copy(d, i):
        there = pair_count - d - 1
        return remote(
            r_out.at[there, i], r_in.at[there, i], x_send.at[there, i], x_recv.at[there, i],
            pair_peer(d),
        )

    load = pltpu.make_async_copy(emb_hbm, emb_ref, load_sem)
    load.start()
    barrier = pltpu.get_barrier_semaphore()
    for d in range(1, seq_count):
        pl.semaphore_signal(barrier, inc=1, device_id=seq_peer(d), device_id_type=MESH)
    for d in range(1, pair_count):
        pl.semaphore_signal(barrier, inc=1, device_id=pair_peer(d), device_id_type=MESH)
    pl.semaphore_signal(barrier, inc=1, device_id={"sub": sibling}, device_id_type=MESH)

    def fill_table(i, carry):
        d, rank = slot_key(i)
        owner = partner(d)

        def look(n, state):
            seen, query, target = state
            query_id = pairs_ref[0, n]
            target_id = pairs_ref[1, n]
            match = lax.div(target_id, prot_dev) == owner
            take = jnp.logical_and(match, seen == rank)
            query = jnp.where(take, query_id, query)
            target = jnp.where(take, target_id, target)
            seen = seen + jnp.where(match, 1, 0)
            return (seen, query, target)

        zero = jnp.int32(0)
        _, query, target = lax.fori_loop(
            0, pair_dev, look, (zero, zero, zero), unroll=pair_dev <= 8
        )
        table[0, i] = query
        table[1, i] = target
        return carry

    lax.fori_loop(0, slots, fill_table, 0)
    pl.semaphore_wait(barrier, seq_count + pair_count - 1)

    for d in range(1, seq_count):
        seq_info_copy(d).start()
    for d in range(1, pair_count):
        pair_info_copy(d).start()
    load.wait()
    for d in range(1, seq_count):
        seq_info_copy(d).wait_recv()

    def send_targets(i, carry):
        d, _ = slot_key(i)
        outgoing[i - capacity] = emb_ref[lax.rem(seq_tables[d - 1, 1, i], prot_dev)]

        @pl.when(i < capacity + window)
        def _():
            z_copy(d, i).start()

        return carry

    lax.fori_loop(capacity, slots, send_targets, 0)
    query_copy().start()
    for d in range(1, pair_count):
        pair_info_copy(d).wait_recv()

    def own_targets(i, carry):
        t_own[i, own_rows, :] = emb_ref[lax.rem(table[1, i], prot_dev)]
        return carry

    lax.fori_loop(0, capacity, own_targets, 0)
    acc[...] = jnp.zeros_like(acc)
    query_copy().wait_recv()

    def sibling_targets(i, carry):
        t_own[i, sibling_rows, :] = emb_other[lax.rem(table[1, i], prot_dev)]
        return carry

    lax.fori_loop(0, capacity, sibling_targets, 0)

    scale = 1.0 / math.sqrt(width)
    contract = (((1,), (1,)), ((), ()))

    def weights(i):
        query_id = table[0, i]
        query = lax.rem(query_id, prot_dev)
        query_length = lengths_ref[query_id]
        target_length = lengths_ref[table[1, i]]
        block = t_own[i]
        own = scale * lax.dot_general(
            emb_ref[query], block, contract, preferred_element_type=jnp.float32
        )
        other = scale * lax.dot_general(
            emb_other[query], block, contract, preferred_element_type=jnp.float32
        )
        rows = lax.broadcasted_iota(jnp.int32, (half, full), 0)
        columns = lax.broadcasted_iota(jnp.int32, (half, full), 1)
        own_live = rows + sub * half < query_length
        other_live = rows + sibling * half < query_length
        col_live = columns < target_length
        col_top = jnp.maximum(
            jnp.max(jnp.where(own_live, own, masked_fill), axis=0, keepdims=True),
            jnp.max(jnp.where(other_live, other, masked_fill), axis=0, keepdims=True),
        )
        own_exp = jnp.where(own_live, jnp.exp(own - col_top), 0.0)
        other_exp = jnp.where(other_live, jnp.exp(other - col_top), 0.0)
        col_total = jnp.sum(own_exp, axis=0, keepdims=True) + jnp.sum(
            other_exp, axis=0, keepdims=True
        )
        masked = jnp.where(col_live, own, masked_fill)
        row_exp = jnp.exp(masked - jnp.max(masked, axis=1, keepdims=True))
        row_total = jnp.sum(row_exp, axis=1, keepdims=True)
        both = row_exp * (0.5 / row_total) + own_exp * (0.5 / col_total)
        return jnp.where(jnp.logical_and(own_live, col_live), both, 0.0).astype(jnp.bfloat16)

    def aligned(weight, i, index):
        return jnp.dot(
            weight, t_own[i, :, feature_block(index)], preferred_element_type=jnp.float32
        )

    def add(result, query_id):
        query = lax.rem(query_id, prot_dev)
        for a in range(prot_dev):
            acc[a] += jnp.where(query == a, result, 0.0)

    def step(i, carry):
        @pl.when(jnp.logical_and(i >= capacity, i < slots))
        def _():
            z_copy(1, i).wait_recv()

            @pl.when(i + window < slots)
            def _():
                z_copy(slot_key(i + window)[0], i + window).start()

            s_copy(i, own_rows).start()

        def tail(k):
            def remote_add(e, inner):
                x_copy(pair_count - 1 - e, k).wait_recv()
                add(r_in[e, k].astype(jnp.float32), pair_tables[e, 0, k])
                return inner

            lax.fori_loop(0, pair_count - 1, remote_add, 0)

        @pl.when(jnp.logical_and(i >= lag, i < slots + lag))
        def _():
            k = i - lag

            @pl.when(k >= capacity)
            def _():
                s_copy(k, sibling_rows).wait_recv()

            weight = weights(k)
            for d in range(1, pair_count):
                there = pair_count - d - 1
                peer = lax.rem(mine + d, pair_count)
                r_out[there, k] = aligned(weight, k, peer).astype(jnp.bfloat16)
                x_copy(d, k).start()
            add(aligned(weight, k, mine), table[0, k])

        @pl.when(i >= lag + 1)
        def _():
            tail(i - lag - 1)

        return carry

    lax.fori_loop(0, slots + lag + 1, step, 0)

    def count(n, counts, ids):
        query = lax.rem(ids(n), prot_dev)
        return tuple(c + jnp.where(query == a, 1, 0) for a, c in enumerate(counts))

    counts = lax.fori_loop(
        0,
        slots,
        lambda n, state: count(n, state, lambda m: table[0, m]),
        (jnp.int32(0),) * prot_dev,
    )
    for e in range(pair_count - 1):
        counts = lax.fori_loop(
            0, slots, lambda n, state: count(n, state, lambda m: pair_tables[e, 0, m]), counts
        )
    for a in range(prot_dev):
        divisor = jnp.maximum(counts[a], 1).astype(jnp.float32)
        out_ref[a] = (acc[a] / divisor).astype(out_ref.dtype)

    for d in range(1, seq_count):
        seq_info_copy(d).wait_send()
    for d in range(1, pair_count):
        pair_info_copy(d).wait_send()
    query_copy().wait_send()

    def finish(i, carry):
        @pl.when(i >= capacity)
        def _():
            z_copy(1, i).wait_send()
            s_copy(i, own_rows).wait_send()

        for d in range(1, pair_count):
            x_copy(d, i).wait_send()
        return carry

    lax.fori_loop(0, slots, finish, 0)


def local(seq_count, pair_count, embeddings, pairs, lengths):
    prot_dev, half, width = embeddings.shape
    pair_dev = pairs.shape[0]
    full = 2 * half
    features = width // pair_count
    capacity = pair_dev // seq_count
    moved = pair_dev - capacity
    others = pair_count - 1
    smem = pl.BlockSpec(memory_space=pltpu.SMEM)
    vmem = pl.BlockSpec(memory_space=pltpu.VMEM)
    dma = pltpu.SemaphoreType.DMA
    bf16 = jnp.bfloat16
    return pl.pallas_call(
        functools.partial(kernel, seq_count, pair_count),
        out_shape=jax.ShapeDtypeStruct((prot_dev, half, features), bf16),
        in_specs=[smem, smem, pl.BlockSpec(memory_space=pl.ANY)],
        out_specs=vmem,
        scratch_shapes=[
            pltpu.SMEM((2, pair_dev), jnp.int32),
            pltpu.SMEM((seq_count - 1, 2, pair_dev), jnp.int32),
            pltpu.SMEM((others, 2, pair_dev), jnp.int32),
            pltpu.VMEM((prot_dev, half, width), bf16),
            pltpu.VMEM((prot_dev, half, width), bf16),
            pltpu.VMEM((moved, half, width), bf16),
            pltpu.VMEM((pair_dev, full, width), bf16),
            pltpu.VMEM((others, pair_dev, half, features), bf16),
            pltpu.VMEM((others, pair_dev, half, features), bf16),
            pltpu.VMEM((prot_dev, half, features), jnp.float32),
            dma,
            dma((seq_count - 1,)),
            dma((seq_count - 1,)),
            dma((others,)),
            dma((others,)),
            dma,
            dma,
            dma((moved,)),
            dma((moved,)),
            dma((moved,)),
            dma((moved,)),
            dma((others, pair_dev)),
            dma((others, pair_dev)),
        ],
        compiler_params=pltpu.CompilerParams(
            collective_id=0, has_side_effects=True, vmem_limit_bytes=60 * 1024 * 1024
        ),
    )(pairs.T, lengths, embeddings)


def solution(mesh):
    placed = (P(("groups", "seq"), "sub", None), P(("groups", "seq", "pair"), None), P("groups"))
    return jax.shard_map(
        functools.partial(local, mesh.shape["seq"], mesh.shape["pair"]),
        mesh=mesh,
        in_specs=placed,
        out_specs=P(("groups", "seq"), "sub", "pair"),
        check_vma=False,
    )
```

time: 76.6 us -> 66 us (0.86)
  the two profiles are of different devices: /device:TPU:28 before, /device:TPU:0 now
where the time goes in v2:
time: 66 us; the launch traced here: 65.7 us
  Pallas kernels  63.4 us (96%)
  local copies, waits for them, and re-layouts  2.26 us (3%)
    pallas_call x1, Pallas kernels, local(): pl.pallas_call(functools.partial(kernel, seq_count, pair_count), out_shap...  63.4 us
    unnamed x1, local copies, waits for them, and re-layouts  2.26 us

profile of v2, /device:TPU:0, one launch (start us, length us, event | category | flops | bytes accessed | tf_op | source)
XLA Modules:
  0.0 65.7 jit_solution(16771704144775225374)
XLA Ops:
  0.0 63.4 %shard_map.37 = bf16[8,128,512]{2,1,0:T(8,128)(2,1)} custom-call(s32[2,8]{1,0:T(2,128)} %bitcast.1, s32[32]{0:T(128)} %lengths_ref.1, bf16[8,128,1024]{2,1,0:T(8,128)(2,1)} %emb_hbm.1), custom_call_target="tpu_custom_call" | custom-call | tf_op jit(solution)/shard_map/pallas_call | solution.py:336
  63.4 2.3 %copy.5 = bf16[8,128,512]{2,1,0:T(8,128)(2,1)} copy(bf16[8,128,512]{2,1,0:T(8,128)(2,1)} %shard_map.37) | data formatting | bytes 2097152

commit v3 on v2

--- a/solution.py
+++ b/solution.py
@@ -9,8 +9,8 @@
 from jax.sharding import PartitionSpec as P
 
 masked_fill = -1e30
-window = 2
-lag = 1
+window = 3
+lag = 0
 shift = 0
 MESH = pl.DeviceIdType.MESH
 
@@ -21,7 +21,7 @@
     pairs_ref,
     lengths_ref,
     emb_hbm,
-    out_ref,
+    out_hbm,
     table,
     seq_tables,
     pair_tables,
@@ -32,6 +32,8 @@
     r_out,
     r_in,
     acc,
+    out_buf,
+    out_sem,
     load_sem,
     seq_info_send,
     seq_info_recv,
@@ -124,6 +126,9 @@
             pair_peer(d),
         )
 
+    def out_copy(a):
+        return pltpu.make_async_copy(out_buf.at[a], out_hbm.at[a], out_sem.at[a])
+
     load = pltpu.make_async_copy(emb_hbm, emb_ref, load_sem)
     load.start()
     barrier = pltpu.get_barrier_semaphore()
@@ -299,8 +304,10 @@
             0, slots, lambda n, state: count(n, state, lambda m: pair_tables[e, 0, m]), counts
         )
     for a in range(prot_dev):
-        divisor = jnp.maximum(counts[a], 1).astype(jnp.float32)
-        out_ref[a] = (acc[a] / divisor).astype(out_ref.dtype)
+        divisor = jnp.full((1, features), jnp.maximum(counts[a], 1).astype(jnp.float32))
+        inverse = 1.0 / divisor
+        out_buf[a] = (acc[a] * inverse).astype(out_buf.dtype)
+        out_copy(a).start()
 
     for d in range(1, seq_count):
         seq_info_copy(d).wait_send()
@@ -319,6 +326,8 @@
         return carry
 
     lax.fori_loop(0, slots, finish, 0)
+    for a in range(prot_dev):
+        out_copy(a).wait()
 
 
 def local(seq_count, pair_count, embeddings, pairs, lengths):
@@ -330,14 +339,13 @@
     moved = pair_dev - capacity
     others = pair_count - 1
     smem = pl.BlockSpec(memory_space=pltpu.SMEM)
-    vmem = pl.BlockSpec(memory_space=pltpu.VMEM)
     dma = pltpu.SemaphoreType.DMA
     bf16 = jnp.bfloat16
     return pl.pallas_call(
         functools.partial(kernel, seq_count, pair_count),
         out_shape=jax.ShapeDtypeStruct((prot_dev, half, features), bf16),
         in_specs=[smem, smem, pl.BlockSpec(memory_space=pl.ANY)],
-        out_specs=vmem,
+        out_specs=pl.BlockSpec(memory_space=pl.ANY),
         scratch_shapes=[
             pltpu.SMEM((2, pair_dev), jnp.int32),
             pltpu.SMEM((seq_count - 1, 2, pair_dev), jnp.int32),
@@ -349,6 +357,8 @@
             pltpu.VMEM((others, pair_dev, half, features), bf16),
             pltpu.VMEM((others, pair_dev, half, features), bf16),
             pltpu.VMEM((prot_dev, half, features), jnp.float32),
+            pltpu.VMEM((prot_dev, half, features), bf16),
+            dma((prot_dev,)),
             dma,
             dma((seq_count - 1,)),
             dma((seq_count - 1,)),

time: 66 us -> 65.5 us (level)
  no operation moved by 1% of the time
where the time goes in v3:
time: 65.5 us; the launch traced here: 65.4 us
  Pallas kernels  63.1 us (96%)
  local copies, waits for them, and re-layouts  2.26 us (3%)
    pallas_call x1, Pallas kernels, local(): pl.pallas_call(functools.partial(kernel, seq_count, pair_count), out_shap...  63.1 us
    unnamed x1, local copies, waits for them, and re-layouts  2.26 us

profile of v3, /device:TPU:0, one launch (start us, length us, event | category | flops | bytes accessed | tf_op | source)
XLA Modules:
  0.0 65.4 jit_solution(1794709721613866716)
XLA Ops:
  0.0 63.1 %shard_map.37 = bf16[8,128,512]{2,1,0:T(8,128)(2,1)} custom-call(s32[2,8]{1,0:T(2,128)} %bitcast.1, s32[32]{0:T(128)} %lengths_ref.1, bf16[8,128,1024]{2,1,0:T(8,128)(2,1)} %emb_hbm.1), custom_call_target="tpu_custom_call" | custom-call | tf_op jit(solution)/shard_map/pallas_call | solution.py:344
  63.1 2.3 %copy.5 = bf16[8,128,512]{2,1,0:T(8,128)(2,1)} copy(bf16[8,128,512]{2,1,0:T(8,128)(2,1)} %shard_map.37) | data formatting | bytes 2097152

commit v4 on v3

--- a/solution.py
+++ b/solution.py
@@ -250,12 +250,11 @@
         @pl.when(jnp.logical_and(i >= capacity, i < slots))
         def _():
             z_copy(1, i).wait_recv()
+            s_copy(i, own_rows).start()
 
             @pl.when(i + window < slots)
             def _():
                 z_copy(slot_key(i + window)[0], i + window).start()
-
-            s_copy(i, own_rows).start()
 
         def tail(k):
             def remote_add(e, inner):

time: 65.5 us -> 65.5 us (level)
  no operation moved by 1% of the time
where the time goes in v4:
time: 65.5 us; the launch traced here: 65.4 us
  Pallas kernels  63.1 us (96%)
  local copies, waits for them, and re-layouts  2.26 us (3%)
    pallas_call x1, Pallas kernels, local(): pl.pallas_call(functools.partial(kernel, seq_count, pair_count), out_shap...  63.1 us
    unnamed x1, local copies, waits for them, and re-layouts  2.26 us

profile of v4, /device:TPU:0, one launch (start us, length us, event | category | flops | bytes accessed | tf_op | source)
XLA Modules:
  0.0 65.4 jit_solution(17762106040660975636)
XLA Ops:
  0.0 63.1 %shard_map.37 = bf16[8,128,512]{2,1,0:T(8,128)(2,1)} custom-call(s32[2,8]{1,0:T(2,128)} %bitcast.1, s32[32]{0:T(128)} %lengths_ref.1, bf16[8,128,1024]{2,1,0:T(8,128)(2,1)} %emb_hbm.1), custom_call_target="tpu_custom_call" | custom-call | tf_op jit(solution)/shard_map/pallas_call | solution.py:343
  63.1 2.3 %copy.5 = bf16[8,128,512]{2,1,0:T(8,128)(2,1)} copy(bf16[8,128,512]{2,1,0:T(8,128)(2,1)} %shard_map.37) | data formatting | bytes 2097152
